TPU v7x, 256 devices: a whole 4x4x8 slice. The times are simulated.
256 devices in a mesh: tensor: 32 (over x, z), dp: 8 (over y, core).
Axes of the slice: x: 4, y: 4, z: 8, core: 2. Of those that a mesh axis runs over, the one named last changes fastest.
Arguments:
- inputs: bfloat16 [256, 128, 28672], P('dp', None, 'tensor'), may hold values from -6 to 6
- out_grads: bfloat16 [256, 128, 8192], P('dp', None, 'tensor'), may hold values from -6 to 6
- proj_in: bfloat16 [28672, 64], P('tensor'), may hold values from -0.03125 to 0.03125
- proj_out: bfloat16 [8192, 64], P('tensor'), may hold values from -0.0625 to 0.0625
- lengths: int32 [256], P('dp'), may hold values from 1 to 128
- queries: bfloat16 [2048, 4096], P(('tensor', 'dp')), may hold values from -0.0078125 to 0.0078125
Outputs:
- scores: float32 [256, 2048], P('dp', 'tensor')
All inputs are finite; a program needn't handle non-finite values.
Results may differ from a plain program's by a relative error of at most 0.005.
Values may be sent and summed in bfloat16 or wider, within the bound.
A program may use at most 64 MiB of HBM per device.

v0:
```python
import jax
import jax.numpy as jnp
from jax import lax
from jax.sharding import PartitionSpec as P


def example_grads(summed, seq_lengths):
    rank_in = summed.shape[2] // 2
    positions = jnp.arange(summed.shape[1], dtype=jnp.int32)
    live_mask = (positions[None, :] < seq_lengths[:, None]).astype(jnp.float32)
    small_a = (summed[:, :, :rank_in] * live_mask[:, :, None]).astype(jnp.bfloat16)
    small_b = summed[:, :, rank_in:].astype(jnp.bfloat16)
    outer = jnp.einsum("sli,slj->sij", small_a, small_b, preferred_element_type=jnp.float32)
    return outer.reshape(summed.shape[0], rank_in * small_b.shape[2]).astype(jnp.bfloat16)


def body(inputs, out_grads, proj_in, proj_out, lengths, queries):
    part_in = jnp.einsum("slk,kr->slr", inputs, proj_in, preferred_element_type=jnp.float32)
    part_out = jnp.einsum("slk,kr->slr", out_grads, proj_out, preferred_element_type=jnp.float32)
    partial_value = jnp.concatenate([part_in, part_out], axis=2)
    query_rows = lax.all_gather(queries, "dp", axis=0, tiled=True)
    totals = lax.psum(partial_value, "tensor")
    grads_all = example_grads(totals, lengths)
    return lax.dot_general(
        grads_all, query_rows, (((1,), (1,)), ((), ())), preferred_element_type=jnp.float32
    )


def solution(mesh):
    return jax.shard_map(
        body,
        mesh=mesh,
        in_specs=(
            P("dp", None, "tensor"),
            P("dp", None, "tensor"),
            P("tensor", None),
            P("tensor", None),
            P("dp"),
            P(("tensor", "dp"), None),
        ),
        out_specs=P("dp", "tensor"),
        check_vma=False,
    )
```

profile of v0, /device:TPU:8, one launch (start us, length us, event | category | flops | bytes accessed | tf_op | source)
XLA Modules:
  0.0 182.0 jit_solution(2219564529039158713)
XLA Ops:
  6.5 0.0 copy-start
  6.5 0.0 copy-start.2
  6.5 0.0 all-reduce.2.cloned.1.call-start
  6.5 5.6 %fusion.3 = f32[32,128,64]{1,2,0:T(8,128)S(1)} fusion(bf16[32,128,896]{2,1,0:T(8,128)(2,1)} %param.6, bf16[896,64]{0,1:T(8,128)(2,1)} %param.8), kind=kOutput, calls=%fused_computation.6 | convolution fusion | flops 469762048 | bytes 8503296 | tf_op jit(solution)/shard_map/slk,kr->slr/dot_general | solution.py:18
  12.1 0.0 copy-done
  12.1 0.0 copy-done.2
  12.1 0.7 fusion.5
  12.9 1.5 pad_maximum_fusion
  14.4 0.0 copy-start.3
  14.4 0.0 copy-start.1
  14.4 0.0 all-reduce.2.cloned.1.call-update
  14.4 0.6 copy-done.3
  15.0 0.1 fusion.7
  15.1 0.1 copy-done.1
  15.2 13.3 %all_gather.3 = bf16[64,4096]{1,0:T(8,128)(2,1)S(1)} all-gather(bf16[8,4096]{1,0:T(8,128)(2,1)S(1)} %copy-done.1), channel_id=1, replica_groups=mesh['tensor'=32,'dp'=8] {'dp'}, dimensions={0}, use_global_device_ids=true | all-gather | bytes 589824 | tf_op jit(solution)/shard_map/all_gather | solution.py:21
  28.5 143.3 %all-reduce.2.cloned.1.call-done = f32[32,128,128]{1,2,0:T(8,128)} async-done(((f32[32,128,128]{1,2,0:T(8,128)}), f32[32,128,128]{1,2,0:T(8,128)}) %all-reduce.2.cloned.1.call-update) | async-done | bytes 2097168 | tf_op jit(solution)/shard_map/psum | solution.py:22
  171.8 1.9 %convolution_convert_fusion = bf16[32,64,64]{2,1,0:T(8,128)(2,1)S(1)} fusion(f32[32,128,128]{1,2,0:T(8,128)} %all-reduce.2.cloned.1.call-done, f32[32,128]{1,0:T(8,128)S(1)} %fusion.7), kind=kOutput, calls=%fused_computation.1 | convolution fusion | flops 34471936 | bytes 2375680 | tf_op jit(solution)/shard_map/sli,slj->sij/dot_general | solution.py:13
  173.8 0.5 convert_element_type.20
  174.2 0.9 fusion.8
Async XLA Ops:
  6.5 5.6 %copy-start = (bf16[32,128,256]{2,1,0:T(8,128)(2,1)S(1)}, bf16[32,128,256]{2,1,0:T(8,128)(2,1)}, u32[]{:S(2)}) copy-start(bf16[32,128,256]{2,1,0:T(8,128)(2,1)} %param.7) | copy-start | bytes 6291460
  6.5 5.6 %copy-start.2 = (bf16[256,64]{0,1:T(8,128)(2,1)S(1)}, bf16[256,64]{0,1:T(8,128)(2,1)}, u32[]{:S(2)}) copy-start(bf16[256,64]{0,1:T(8,128)(2,1)} %param.9) | copy-start | bytes 98308
  6.5 165.3 %all-reduce.2.cloned.1.call-start = ((), (), s32[]{:S(2)}) async-start(), calls=%async_computation | async-start | bytes 4194304 | tf_op jit(solution)/shard_map/psum | solution.py:22
  14.4 0.7 copy-start.3
  14.4 0.9 copy-start.1
Sparse Core Ops, SparseCore 0:
  14.5 157.2 all-reduce.1
where the time goes:
time: 182 us
  waiting for transfers between devices  143 us (79%)
  between operations  13.4 us (7%)
  blocking collectives  13.3 us (7%)
  matrix products  9.14 us (5%)
    psum x1, waiting for transfers between devices, body(): totals = lax.psum(partial_value, 'tensor')  143 us
    all_gather x1, blocking collectives, body(): query_rows = lax.all_gather(queries, 'dp', axis=0, tiled=True)  13.3 us
    dot_general x1, matrix products, body(): jnp.einsum('slk,kr->slr', inputs, proj_in, preferred_element_type=jnp.flo...  5.58 us
  transfers between devices with their start and end apart: 1, of which 1 were waited for; matrix products, arithmetic and copies ran while one was open for 0% of the time, Pallas kernels for 0%

commit v1 on v0

v1 whole, which is shorter than its diff:
```python
import functools

import jax
import jax.numpy as jnp
from jax import lax
from jax.experimental import pallas as pl
from jax.experimental.pallas import tpu as pltpu
from jax.sharding import PartitionSpec as P

MESH = pl.DeviceIdType.MESH
F32 = jnp.float32
BF16 = jnp.bfloat16
NX = 4


def encode(value):
    return (value * jnp.abs(value)).astype(BF16)


def decode(code):
    wide = code.astype(F32)
    root = jnp.sqrt(jnp.abs(wide))
    return jnp.where(wide < 0, -root, root)


def split(value):
    high = value.astype(BF16)
    return high, (value - high.astype(F32)).astype(BF16)


def kernel(
    nz, nd,
    x_hbm, g_hbm, wi_hbm, wo_hbm, len_ref, q_hbm, out_ref,
    xbuf, gbuf, wi, wo, w, raw, comb, keep, chain_in, final_in, z_out, z_in, qall, qflat, exall, exwide, small,
    load_sem, w_sem, raw_send, comb_send, chain_recv, final_recv, z_send, z_recv,
    q_send, q_recv, q_local, ex_send, ex_recv, fw_send,
):
    half = nz // 2
    tokens, rank = x_hbm.shape[1], wi_hbm.shape[1]
    feats = x_hbm.shape[2]
    t = lax.axis_index("tensor")
    d = lax.axis_index("dp")
    x, z = t // nz, t % nz
    x_right, x_left, x_far = (x + 1) % NX, (x + NX - 1) % NX, (x + 2) % NX
    right, left, far = x_right * nz + z, x_left * nz + z, x_far * nz + z

    def at_x(index):
        return {"tensor": index, "dp": d}

    def peer_z(k):
        return x * nz + (z + k) % nz

    barrier = pltpu.get_barrier_semaphore()
    partners = [at_x(right), at_x(left), at_x(far)]
    partners += [at_x(peer_z(k)) for k in range(1, nz)]
    partners += [{"tensor": t, "dp": (d + k) % nd} for k in range(1, nd)]
    for partner in partners:
        pl.semaphore_signal(barrier, inc=1, device_id=partner, device_id_type=MESH)

    w_copies = [
        pltpu.make_async_copy(wi_hbm, wi, w_sem.at[0]),
        pltpu.make_async_copy(wo_hbm, wo, w_sem.at[1]),
    ]
    for copy in w_copies:
        copy.start()

    loads = []
    for i in range(half):
        even, odd = (z + half + i) % nz, (z + half - 1 - i) % nz
        order = [
            (x_far, even), (x_far, odd), (x_right, odd), (x_left, even),
            (x_right, even), (x_left, odd), (x, even), (x, odd),
        ]
        for k, (xd, zd) in enumerate(order):
            slot = i * 8 + k
            s = xd * nz + zd
            loads.append((
                pltpu.make_async_copy(x_hbm.at[s], xbuf.at[slot], load_sem.at[0, slot]),
                pltpu.make_async_copy(g_hbm.at[s], gbuf.at[slot], load_sem.at[1, slot]),
            ))
            for copy in loads[-1]:
                copy.start()
    own_q = pltpu.make_async_copy(q_hbm, qall.at[d], q_local)
    own_q.start()

    for copy in w_copies:
        copy.wait()
    w[0:feats, :] = jnp.concatenate([wi[...], jnp.zeros_like(wi)], axis=1)
    w[feats:, :] = jnp.concatenate([jnp.zeros_like(wo), wo[...]], axis=1)

    def project(i, group):
        first = i * 8 + group * 4
        for slot in range(first, first + 4):
            for copy in loads[slot]:
                copy.wait()
        xs = xbuf[first:first + 4].reshape(4 * tokens, feats)
        gs = gbuf[first:first + 4].reshape(4 * tokens, gbuf.shape[2])
        total = jnp.dot(xs, w[0:feats, :], preferred_element_type=F32)
        total += jnp.dot(gs, w[feats:, :], preferred_element_type=F32)
        return total.reshape(4, tokens, 2 * rank)

    def remote(src, dst, send, recv, device):
        return pltpu.make_async_remote_copy(
            src_ref=src, dst_ref=dst, send_sem=send, recv_sem=recv, device_id=device, device_id_type=MESH
        )

    raw_copies, comb_copies = {}, {}

    def first_sends(i):
        raw[i] = encode(project(i, 0))
        raw_copies[i] = [
            remote(raw.at[i, 0], chain_in.at[0, i], raw_send.at[i, 0], chain_recv.at[0, i], at_x(right)),
            remote(raw.at[i, 1], chain_in.at[1, i], raw_send.at[i, 1], chain_recv.at[1, i], at_x(left)),
            remote(raw.at[i, 2], final_in.at[0, i, 1], raw_send.at[i, 2], final_recv.at[0, i, 1], at_x(right)),
            remote(raw.at[i, 3], final_in.at[1, i, 0], raw_send.at[i, 3], final_recv.at[1, i, 0], at_x(left)),
        ]
        for copy in raw_copies[i]:
            copy.start()

    def combine(i):
        comb_copies[i] = []
        for side in range(2):
            raw_copies[i][side].wait_recv()
            comb[i, side] = encode(keep[i, side] + decode(chain_in[side, i]))
            copy = remote(
                comb.at[i, side], final_in.at[side, i, side], comb_send.at[i, side], final_recv.at[side, i, side],
                at_x(right if side == 0 else left),
            )
            copy.start()
            comb_copies[i].append(copy)

    z_copies = {}

    def reduce_x(i):
        for parity in range(2):
            k = half + i if parity == 0 else half - 1 - i
            comb_copies[i][parity].wait_recv()
            raw_copies[i][3 - parity].wait_recv()
            total = keep[i, 2 + parity] + decode(final_in[0, i, parity]) + decode(final_in[1, i, parity])
            if k == 0:
                keep[i, 2 + parity] = total
                continue
            z_out[k - 1] = encode(total)
            z_copies[k] = remote(
                z_out.at[k - 1], z_in.at[k - 1], z_send.at[k - 1], z_recv.at[k - 1], at_x(peer_z(k))
            )
            z_copies[k].start()

    q_copies = []
    for i in range(half + 2):
        if i == 0:
            raw_first = None
            pl.semaphore_wait(barrier, len(partners))
        if i < half:
            first_sends(i)
        if i == 0:
            for k in range(1, nd):
                copy = remote(
                    q_hbm, qall.at[d], q_send.at[k - 1], q_recv.at[k - 1], {"tensor": t, "dp": (d + k) % nd}
                )
                copy.start()
                q_copies.append(copy)
        if 1 <= i <= half:
            combine(i - 1)
        if i < half:
            keep[i] = project(i, 1)
        if i >= 2:
            reduce_x(i - 2)

    own_q.wait()
    for copy in q_copies:
        copy.wait()
    for k in range(nd):
        small_rows = qall.shape[1]
        if k % 2 == 0:
            qflat[k * small_rows:(k + 2) * small_rows, :] = jnp.concatenate([qall[k], qall[k + 1]], axis=0)

    total = keep[half - 1, 3]
    for i in range(half):
        for k in (half + i, half - 1 - i):
            if k > 0:
                z_copies[k].wait_recv()
                total += decode(z_in[k - 1])

    live = (lax.broadcasted_iota(jnp.int32, (tokens, 2 * rank), 0) < len_ref[t]).astype(F32)
    lane = lax.broadcasted_iota(jnp.int32, (tokens, 2 * rank), 1)
    both = jnp.where(lane < rank, pltpu.roll(total, rank, 1), total)
    a_high, a_low = split(total * live)
    b_high, b_low = split(both)

    def outer(left_side, right_side):
        return lax.dot_general(left_side, right_side, (((0,), (0,)), ((), ())), preferred_element_type=F32)

    small[...] = (outer(a_high, b_high) + (outer(a_high, b_low) + outer(a_low, b_high)))[0:rank]
    rows = rank // 2
    lane_half = lax.broadcasted_iota(jnp.int32, (rows, 2 * rank), 1)
    example = jnp.where(lane_half < rank, small[pl.ds(0, rows, stride=2), :], small[pl.ds(1, rows, stride=2), :])
    exall[t] = example.astype(BF16)

    ex_copies = []
    for k in range(1, nz):
        copy = remote(exall.at[t], exall.at[t], ex_send.at[k - 1], ex_recv.at[0, k], at_x(peer_z(k)))
        copy.start()
        ex_copies.append(copy)
    fw_copies = []
    for j, k in enumerate([0] + [k for m in range(1, half + 1) for k in ((m, nz - m) if m < half else (m,))]):
        source = x * nz + (z + nz - k) % nz
        if k > 0:
            ex_copies[k - 1].wait_recv()
        for side, device in enumerate((right, left, far)):
            copy = remote(
                exall.at[source], exall.at[source], fw_send.at[side, k], ex_recv.at[1 + side, k], at_x(device)
            )
            copy.start()
            fw_copies.append(copy)
    for copy in fw_copies:
        copy.wait_recv()

    count = exall.shape[0]
    exwide[...] = exall[...].reshape(count * rows, 2 * rank).astype(F32)
    flat = jnp.concatenate([exwide[pl.ds(r, count, stride=rows), :] for r in range(rows)], axis=1)
    out_ref[...] = lax.dot_general(
        flat.astype(BF16), qflat[...], (((1,), (1,)), ((), ())), preferred_element_type=F32
    )

    for copies in list(raw_copies.values()) + list(comb_copies.values()):
        for copy in copies:
            copy.wait_send()
    for copy in list(z_copies.values()) + ex_copies + fw_copies:
        copy.wait_send()


def solution(mesh):
    nt, nd = mesh.shape["tensor"], mesh.shape["dp"]
    nz = nt // NX
    half = nz // 2

    def body(inputs, out_grads, proj_in, proj_out, lengths, queries):
        seqs, tokens, feats = inputs.shape
        grads = out_grads.shape[2]
        rank = proj_in.shape[1]
        lanes = 2 * rank
        block = (tokens, lanes)
        dma = pltpu.SemaphoreType.DMA
        return pl.pallas_call(
            functools.partial(kernel, nz, nd),
            out_shape=jax.ShapeDtypeStruct((seqs, nd * queries.shape[0]), F32),
            in_specs=[
                pl.BlockSpec(memory_space=pl.ANY),
                pl.BlockSpec(memory_space=pl.ANY),
                pl.BlockSpec(memory_space=pl.ANY),
                pl.BlockSpec(memory_space=pl.ANY),
                pl.BlockSpec(memory_space=pltpu.SMEM),
                pl.BlockSpec(memory_space=pl.ANY),
            ],
            out_specs=pl.BlockSpec(memory_space=pltpu.VMEM),
            scratch_shapes=[
                pltpu.VMEM((seqs, tokens, feats), BF16),
                pltpu.VMEM((seqs, tokens, grads), BF16),
                pltpu.VMEM((feats, rank), BF16),
                pltpu.VMEM((grads, rank), BF16),
                pltpu.VMEM((feats + grads, lanes), BF16),
                pltpu.VMEM((half, 4) + block, BF16),
                pltpu.VMEM((half, 2) + block, BF16),
                pltpu.VMEM((half, 4) + block, F32),
                pltpu.VMEM((2, half) + block, BF16),
                pltpu.VMEM((2, half, 2) + block, BF16),
                pltpu.VMEM((nz - 1,) + block, BF16),
                pltpu.VMEM((nz - 1,) + block, BF16),
                pltpu.VMEM((nd,) + queries.shape, BF16),
                pltpu.VMEM((nd * queries.shape[0], queries.shape[1]), BF16),
                pltpu.VMEM((seqs, rank // 2, lanes), BF16),
                pltpu.VMEM((seqs * rank // 2, lanes), F32),
                pltpu.VMEM((rank, lanes), F32),
                dma((2, seqs)),
                dma((2,)),
                dma((half, 4)),
                dma((half, 2)),
                dma((2, half)),
                dma((2, half, 2)),
                dma((nz - 1,)),
                dma((nz - 1,)),
                dma((nd - 1,)),
                dma((nd - 1,)),
                dma,
                dma((nz - 1,)),
                dma((4, nz)),
                dma((3, nz)),
            ],
            compiler_params=pltpu.CompilerParams(
                collective_id=0, has_side_effects=True, vmem_limit_bytes=48 * 1024 * 1024
            ),
        )(inputs, out_grads, proj_in, proj_out, lengths, queries)

    return jax.shard_map(
        body,
        mesh=mesh,
        in_specs=(
            P("dp", None, "tensor"),
            P("dp", None, "tensor"),
            P("tensor", None),
            P("tensor", None),
            P("dp"),
            P(("tensor", "dp"), None),
        ),
        out_specs=P("dp", "tensor"),
        check_vma=False,
    )
```

time: 182 us -> 44.2 us (0.24)
  waiting for transfers between devices: 143 us -> 0 us
  Pallas kernels: 0 us -> 38.3 us
  between operations: 13.4 us -> 0.03 us
  blocking collectives: 13.3 us -> 0 us
  matrix products: 9.14 us -> 0 us
  local copies, waits for them, and re-layouts: 1.23 us -> 5.63 us
    psum x1 -> x0, waiting for transfers between devices: 143 us -> none  [body(): totals = lax.psum(partial_value, 'tensor')]
    pallas_call x0 -> x1, Pallas kernels: none -> 38.3 us  [body(): pl.pallas_call(functools.partial(kernel, nz, nd), out_shape=jax.ShapeDtyp...]
    all_gather x1 -> x0, blocking collectives: 13.3 us -> none  [body(): query_rows = lax.all_gather(queries, 'dp', axis=0, tiled=True)]
    dot_general x4 -> x0, matrix products: 9.14 us -> none  [the longest x1 5.58 us: body(): jnp.einsum('slk,kr->slr', inputs, proj_in, preferred_element_type=jnp.flo...]
    unnamed x8 -> x9, local copies, waits for them, and re-layouts: 0.77 us -> 5.63 us
  transfers between devices with their start and end apart: 1 -> 0, of which waited for: 1 -> 0; matrix products, arithmetic and copies ran while one was open for 0% -> 0% of each run, Pallas kernels for 0% -> 0%
where the time goes in v1:
time: 44.2 us; the launch traced here: 43.9 us
  Pallas kernels  38.3 us (87%)
  local copies, waits for them, and re-layouts  5.63 us (13%)
    pallas_call x1, Pallas kernels, body(): pl.pallas_call(functools.partial(kernel, nz, nd), out_shape=jax.ShapeDtyp...  38.3 us
    unnamed x9, local copies, waits for them, and re-layouts  5.63 us

profile of v1, /device:TPU:8, one launch (start us, length us, event | category | flops | bytes accessed | tf_op | source)
XLA Modules:
  0.0 43.9 jit_solution(2419318679610830139)
XLA Ops:
  0.0 0.9 %copy.8.wo_hbm = bf16[256,64]{1,0:T(8,128)(2,1)S(1)} copy(bf16[256,64]{0,1:T(8,128)(2,1)} %param.9) | data formatting | bytes 65536 | tf_op args[3]
  0.9 1.1 %copy.7.wi_hbm = bf16[896,64]{1,0:T(8,128)(2,1)S(1)} copy(bf16[896,64]{0,1:T(8,128)(2,1)} %param.8) | data formatting | bytes 229376 | tf_op args[2]
  1.9 0.0 copy-start
  2.0 1.6 %copy-done = bf16[32,128,256]{2,1,0:T(8,128)(2,1)S(1)} copy-done((bf16[32,128,256]{2,1,0:T(8,128)(2,1)S(1)}, bf16[32,128,256]{2,1,0:T(8,128)(2,1)}, u32[]{:S(2)}) %copy-start) | copy-done | bytes 2097176
  3.5 0.0 copy-start.1
  3.5 0.8 %copy-done.1 = bf16[8,4096]{1,0:T(8,128)(2,1)S(1)} copy-done((bf16[8,4096]{1,0:T(8,128)(2,1)S(1)}, bf16[8,4096]{1,0:T(8,128)(2,1)}, u32[]{:S(2)}) %copy-start.1) | copy-done | bytes 65560
  4.4 0.0 copy-start.2
  4.4 0.7 %copy-done.2 = s32[32]{0:T(128)S(1)} copy-done((s32[32]{0:T(128)S(1)}, s32[32]{0:T(128)}, u32[]{:S(2)}) %copy-start.2) | copy-done | bytes 152
  5.0 38.3 %shard_map.64 = f32[32,64]{1,0:T(8,128)S(1)} custom-call(bf16[32,128,896]{2,1,0:T(8,128)(2,1)} %x_hbm.1, bf16[32,128,256]{2,1,0:T(8,128)(2,1)S(1)} %copy-done, bf16[896,64]{1,0:T(8,128)(2,1)S(1)} %copy.7.wi_hbm, bf16[256,64]{1,0:T(8,128)(2,1)S(1)} %copy.8.wo_hbm, s32[32]{0:T(128)S(1)} %copy-done.2, bf16[8,4096]{1,0:T(8,128)(2,1)S(1)} %copy-done.1), custom_call_target="tpu_custom_call" | custom-call | tf_op jit(solution)/shard_map/pallas_call | solution.py:245
  43.3 0.6 %copy.10 = f32[32,64]{1,0:T(8,128)} copy(f32[32,64]{1,0:T(8,128)S(1)} %shard_map.64) | data formatting | bytes 16384
Async XLA Ops:
  1.9 1.6 %copy-start = (bf16[32,128,256]{2,1,0:T(8,128)(2,1)S(1)}, bf16[32,128,256]{2,1,0:T(8,128)(2,1)}, u32[]{:S(2)}) copy-start(bf16[32,128,256]{2,1,0:T(8,128)(2,1)} %g_hbm.1) | copy-start | bytes 6291460
  3.5 0.8 %copy-start.1 = (bf16[8,4096]{1,0:T(8,128)(2,1)S(1)}, bf16[8,4096]{1,0:T(8,128)(2,1)}, u32[]{:S(2)}) copy-start(bf16[8,4096]{1,0:T(8,128)(2,1)} %q_hbm.1) | copy-start | bytes 196612
  4.4 0.7 %copy-start.2 = (s32[32]{0:T(128)S(1)}, s32[32]{0:T(128)}, u32[]{:S(2)}) copy-start(s32[32]{0:T(128)} %len_ref.1) | copy-start | bytes 388

commit v2 on v0

v2 whole, which is shorter than its diff:
```python
import functools

import jax
import jax.numpy as jnp
from jax import lax
from jax.experimental import pallas as pl
from jax.experimental.pallas import tpu as pltpu
from jax.sharding import PartitionSpec as P

MESH = pl.DeviceIdType.MESH
F32 = jnp.float32
BF16 = jnp.bfloat16
NX = 4


def encode(value):
    return (value * jnp.abs(value)).astype(BF16)


def decode(code):
    wide = code.astype(F32)
    root = jnp.sqrt(jnp.abs(wide))
    return jnp.where(wide < 0, -root, root)


def split(value):
    high = value.astype(BF16)
    return high, (value - high.astype(F32)).astype(BF16)


def hops(steps, size):
    return min(steps, size - steps)


def kernel(
    nz, nd,
    x_hbm, g_hbm, wi_hbm, wo_hbm, len_hbm, q_hbm, out_ref,
    acts, wt, w, len_ref, sent, keep, chain_in, final_in, z_out, z_in, qall, qflat, exall, exwide, small,
    load_sem, w_sem, len_sem, own_q_sem, x_send, z_send, q_send, ex_send, chain_recv, final_recv, z_recv, q_recv, ex_recv,
):
    half = nz // 2
    tokens, rank = x_hbm.shape[1], wi_hbm.shape[0]
    feats = x_hbm.shape[2]
    t = lax.axis_index("tensor")
    d = lax.axis_index("dp")
    x, z = t // nz, t % nz
    x_right, x_left, x_far = (x + 1) % NX, (x + NX - 1) % NX, (x + 2) % NX

    def peer(dx, dz):
        return {"tensor": ((x + dx) % NX) * nz + (z + dz) % nz, "dp": d}

    right, left = peer(1, 0), peer(NX - 1, 0)
    barrier = pltpu.get_barrier_semaphore()
    partners = [right, left]
    partners += [peer(0, k) for k in range(1, nz)]
    partners += [{"tensor": t, "dp": (d + k) % nd} for k in range(1, nd)]
    for partner in partners:
        pl.semaphore_signal(barrier, inc=1, device_id=partner, device_id_type=MESH)

    offsets = [(half + i, half - 1 - i) for i in range(half)]
    first_group, second_group = [], []
    for even, odd in offsets:
        ze, zo = (z + even) % nz, (z + odd) % nz
        first_group.append([(x_far, ze), (x_far, zo), (x_right, zo), (x_left, ze)])
        second_group.append([(x_right, ze), (x_left, zo), (x, ze), (x, zo)])

    wt[...] = jnp.zeros_like(wt)
    pltpu.make_async_copy(wi_hbm, wt.at[0:rank, 0:feats], w_sem).start()
    pltpu.make_async_copy(wo_hbm, wt.at[rank:2 * rank, feats:], w_sem).start()
    for group, owners in enumerate(first_group + second_group):
        for k, (xd, zd) in enumerate(owners):
            s, slot = xd * nz + zd, group * 4 + k
            pltpu.make_async_copy(x_hbm.at[s], acts.at[slot, :, 0:feats], load_sem.at[group]).start()
            pltpu.make_async_copy(g_hbm.at[s], acts.at[slot, :, feats:], load_sem.at[group]).start()
    own_q = pltpu.make_async_copy(q_hbm, qall.at[d], own_q_sem)
    own_q.start()
    own_len = pltpu.make_async_copy(len_hbm, len_ref, len_sem)
    own_len.start()

    def drain(ref, sem):
        pltpu.make_async_copy(ref, ref, sem).wait()

    drain(wt.at[0:rank], w_sem)
    w[...] = wt[...].T

    def project(group):
        block = acts.at[group * 4:group * 4 + 4]
        drain(block, load_sem.at[group])
        rows = block[...].reshape(4 * tokens, block.shape[2])
        return jnp.dot(rows, w[...], preferred_element_type=F32).reshape(4, tokens, 2 * rank)

    def send(src, dst, send_sem, recv_sem, device):
        pltpu.make_async_remote_copy(
            src_ref=src, dst_ref=dst, send_sem=send_sem, recv_sem=recv_sem, device_id=device, device_id_type=MESH
        ).start()

    def send_far(i):
        for side, device in enumerate((right, left)):
            send(sent.at[i, side], chain_in.at[i, side], x_send, chain_recv.at[i, side], device)

    def send_raw(i):
        send(sent.at[i, 2], final_in.at[i, 1, 0], x_send, final_recv.at[i], right)
        send(sent.at[i, 3], final_in.at[i, 0, 1], x_send, final_recv.at[i], left)

    def combine(i):
        for side, device in enumerate((right, left)):
            drain(chain_in.at[i, side], chain_recv.at[i, side])
            sent[i, 4 + side] = encode(keep[i, side] + decode(chain_in[i, side]))
            send(sent.at[i, 4 + side], final_in.at[i, side, side], x_send, final_recv.at[i], device)

    def reduce_x(i):
        drain(final_in.at[i], final_recv.at[i])
        for parity, k in enumerate(offsets[i]):
            total = keep[i, 2 + parity] + (decode(final_in[i, parity, 0]) + decode(final_in[i, parity, 1]))
            if k == 0:
                return total
            z_out[k - 1] = encode(total)
            send(z_out.at[k - 1], z_in.at[k - 1], z_send, z_recv, peer(0, k))

    for i in range(half):
        sent[i, 0:4] = encode(project(i))
    pl.semaphore_wait(barrier, len(partners))
    send_far(0)
    if half > 1:
        send_far(1)
    send_raw(0)
    for i in range(2, half):
        send_far(i)
        send_raw(i - 1)
    for i in range(half):
        keep[i] = project(half + i)
        combine(i)
        if i == 0 and half > 1:
            send_raw(half - 1)
        if i == 0:
            for k in range(1, nd):
                send(q_hbm, qall.at[d], q_send, q_recv, {"tensor": t, "dp": (d + k) % nd})
    for i in range(half):
        total = reduce_x(i)

    own_q.wait()
    own_len.wait()
    drain(qall.at[0:nd - 1], q_recv)
    rows = qall.shape[1]
    for k in range(0, nd, 2):
        qflat[k * rows:(k + 2) * rows, :] = jnp.concatenate([qall[k], qall[k + 1]], axis=0)

    drain(z_in, z_recv)
    for k in range(nz - 1):
        total += decode(z_in[k])

    live = (lax.broadcasted_iota(jnp.int32, (tokens, 2 * rank), 0) < len_ref[t]).astype(F32)
    lane = lax.broadcasted_iota(jnp.int32, (tokens, 2 * rank), 1)
    both = jnp.where(lane < rank, pltpu.roll(total, rank, 1), total)
    a_high, a_low = split(total * live)
    b_high, b_low = split(both)

    def outer(left_side, right_side):
        return lax.dot_general(left_side, right_side, (((0,), (0,)), ((), ())), preferred_element_type=F32)

    small[...] = (outer(a_high, b_high) + (outer(a_high, b_low) + outer(a_low, b_high)))[0:rank]
    pairs = rank // 2
    lane_half = lax.broadcasted_iota(jnp.int32, (pairs, 2 * rank), 1)
    example = jnp.where(lane_half < rank, small[pl.ds(0, pairs, stride=2), :], small[pl.ds(1, pairs, stride=2), :])
    exall[t] = example.astype(BF16)

    others = [(dx, dz) for dx in range(NX) for dz in range(nz) if (dx, dz) != (0, 0)]
    others.sort(key=lambda step: -(hops(step[0], NX) + hops(step[1], nz)))
    for dx, dz in others:
        send(exall.at[t], exall.at[t], ex_send, ex_recv, peer(dx, dz))
    count = exall.shape[0]
    drain(exall.at[0:count - 1], ex_recv)

    exwide[...] = exall[...].reshape(count * pairs, 2 * rank).astype(F32)
    flat = jnp.concatenate([exwide[pl.ds(r, count, stride=pairs), :] for r in range(pairs)], axis=1)
    out_ref[...] = lax.dot_general(
        flat.astype(BF16), qflat[...], (((1,), (1,)), ((), ())), preferred_element_type=F32
    )

    drain(sent, x_send)
    drain(z_out, z_send)
    drain(qall.at[0:nd - 1], q_send)
    drain(exall.at[0:count - 1], ex_send)


def solution(mesh):
    nt, nd = mesh.shape["tensor"], mesh.shape["dp"]
    nz = nt // NX
    half = nz // 2

    def body(inputs, out_grads, proj_in, proj_out, lengths, queries):
        seqs, tokens, feats = inputs.shape
        grads = out_grads.shape[2]
        rank = proj_in.shape[1]
        lanes = 2 * rank
        block = (tokens, lanes)
        dma = pltpu.SemaphoreType.DMA
        return pl.pallas_call(
            functools.partial(kernel, nz, nd),
            out_shape=jax.ShapeDtypeStruct((seqs, nd * queries.shape[0]), F32),
            in_specs=[pl.BlockSpec(memory_space=pltpu.HBM)] * 6,
            out_specs=pl.BlockSpec(memory_space=pltpu.VMEM),
            scratch_shapes=[
                pltpu.VMEM((seqs, tokens, feats + grads), BF16),
                pltpu.VMEM((lanes, feats + grads), BF16),
                pltpu.VMEM((feats + grads, lanes), BF16),
                pltpu.SMEM(lengths.shape, jnp.int32),
                pltpu.VMEM((half, 6) + block, BF16),
                pltpu.VMEM((half, 4) + block, F32),
                pltpu.VMEM((half, 2) + block, BF16),
                pltpu.VMEM((half, 2, 2) + block, BF16),
                pltpu.VMEM((nz - 1,) + block, BF16),
                pltpu.VMEM((nz - 1,) + block, BF16),
                pltpu.VMEM((nd,) + queries.shape, BF16),
                pltpu.VMEM((nd * queries.shape[0], queries.shape[1]), BF16),
                pltpu.VMEM((seqs, rank // 2, lanes), BF16),
                pltpu.VMEM((seqs * rank // 2, lanes), F32),
                pltpu.VMEM((rank, lanes), F32),
                dma((nz,)),
            ] + [dma] * 7 + [dma((half, 2)), dma((half,))] + [dma] * 3,
            compiler_params=pltpu.CompilerParams(
                collective_id=0, has_side_effects=True, vmem_limit_bytes=60 * 1024 * 1024
            ),
        )(inputs, out_grads, proj_in.T, proj_out.T, lengths, queries)

    return jax.shard_map(
        body,
        mesh=mesh,
        in_specs=(
            P("dp", None, "tensor"),
            P("dp", None, "tensor"),
            P("tensor", None),
            P("tensor", None),
            P("dp"),
            P(("tensor", "dp"), None),
        ),
        out_specs=P("dp", "tensor"),
        check_vma=False,
    )
```

time: 182 us -> 37.4 us (0.21)
  waiting for transfers between devices: 143 us -> 0 us
  Pallas kernels: 0 us -> 35.9 us
  between operations: 13.4 us -> 0.01 us
  blocking collectives: 13.3 us -> 0 us
  matrix products: 9.14 us -> 0 us
    psum x1 -> x0, waiting for transfers between devices: 143 us -> none  [body(): totals = lax.psum(partial_value, 'tensor')]
    pallas_call x0 -> x1, Pallas kernels: none -> 35.9 us  [body(): pl.pallas_call(functools.partial(kernel, nz, nd), out_shape=jax.ShapeDtyp...]
    all_gather x1 -> x0, blocking collectives: 13.3 us -> none  [body(): query_rows = lax.all_gather(queries, 'dp', axis=0, tiled=True)]
    dot_general x4 -> x0, matrix products: 9.14 us -> none  [the longest x1 5.58 us: body(): jnp.einsum('slk,kr->slr', inputs, proj_in, preferred_element_type=jnp.flo...]
  transfers between devices with their start and end apart: 1 -> 0, of which waited for: 1 -> 0; matrix products, arithmetic and copies ran while one was open for 0% -> 0% of each run, Pallas kernels for 0% -> 0%
where the time goes in v2:
time: 37.4 us; the launch traced here: 37.3 us
  Pallas kernels  35.9 us (96%)
  local copies, waits for them, and re-layouts  1.32 us (4%)
    pallas_call x1, Pallas kernels, body(): pl.pallas_call(functools.partial(kernel, nz, nd), out_shape=jax.ShapeDtyp...  35.9 us
    unnamed x1, local copies, waits for them, and re-layouts  1.32 us

profile of v2, /device:TPU:8, one launch (start us, length us, event | category | flops | bytes accessed | tf_op | source)
XLA Modules:
  0.0 37.3 jit_solution(6954415483349276515)
XLA Ops:
  0.0 35.9 %shard_map.64 = f32[32,64]{1,0:T(8,128)} custom-call(bf16[32,128,896]{2,1,0:T(8,128)(2,1)} %x_hbm.1, bf16[32,128,256]{2,1,0:T(8,128)(2,1)} %g_hbm.1, bf16[64,896]{1,0:T(8,128)(2,1)} %bitcast.2, bf16[64,256]{1,0:T(8,128)(2,1)} %bitcast.3, s32[32]{0:T(128)} %len_hbm.1, bf16[8,4096]{1,0:T(8,128)(2,1)} %q_hbm.1), custom_call_target="tpu_custom_call" | custom-call | tf_op jit(solution)/shard_map/pallas_call | solution.py:198
  35.9 1.3 %copy.8 = f32[32,64]{1,0:T(8,128)} copy(f32[32,64]{1,0:T(8,128)} %shard_map.64) | data formatting | bytes 16384

commit v3 on v2

--- a/solution.py
+++ b/solution.py
@@ -36,7 +36,7 @@
     nz, nd,
     x_hbm, g_hbm, wi_hbm, wo_hbm, len_hbm, q_hbm, out_ref,
     acts, wt, w, len_ref, sent, keep, chain_in, final_in, z_out, z_in, qall, qflat, exall, exwide, small,
-    load_sem, w_sem, len_sem, own_q_sem, x_send, z_send, q_send, ex_send, chain_recv, final_recv, z_recv, q_recv, ex_recv,
+    load_sem, w_sem, len_sem, own_q_sem, in_sem, x_send, z_send, q_send, ex_send, chain_recv, final_recv, z_recv, q_recv, ex_recv,
 ):
     half = nz // 2
     tokens, rank = x_hbm.shape[1], wi_hbm.shape[0]
@@ -50,28 +50,43 @@
         return {"tensor": ((x + dx) % NX) * nz + (z + dz) % nz, "dp": d}
 
     right, left = peer(1, 0), peer(NX - 1, 0)
+    core, y, ny = d % 2, d // 2, nd // 2
+
+    def peer_y(dy, side):
+        return {"tensor": t, "dp": ((y + dy) % ny) * 2 + side}
+
     barrier = pltpu.get_barrier_semaphore()
     partners = [right, left]
     partners += [peer(0, k) for k in range(1, nz)]
-    partners += [{"tensor": t, "dp": (d + k) % nd} for k in range(1, nd)]
+    partners += [peer_y(k, core) for k in range(1, ny)]
     for partner in partners:
         pl.semaphore_signal(barrier, inc=1, device_id=partner, device_id_type=MESH)
 
+    @pl.when(core == 0)
+    def _():
+        for k in range(ny):
+            pl.semaphore_signal(barrier, inc=1, device_id=peer_y(k, 1), device_id_type=MESH)
+
     offsets = [(half + i, half - 1 - i) for i in range(half)]
-    first_group, second_group = [], []
-    for even, odd in offsets:
+    chunks = [[], [], [], [], [], []]
+    early = (half + 1) // 2
+    for i, (even, odd) in enumerate(offsets):
         ze, zo = (z + even) % nz, (z + odd) % nz
-        first_group.append([(x_far, ze), (x_far, zo), (x_right, zo), (x_left, ze)])
-        second_group.append([(x_right, ze), (x_left, zo), (x, ze), (x, zo)])
+        chunks[0 if i < early else 2] += [(x_far, ze), (x_far, zo)]
+        chunks[1 if i < early else 4] += [(x_right, zo), (x_left, ze)]
+        chunks[3] += [(x_right, ze), (x_left, zo)]
+        chunks[5] += [(x, ze), (x, zo)]
 
     wt[...] = jnp.zeros_like(wt)
     pltpu.make_async_copy(wi_hbm, wt.at[0:rank, 0:feats], w_sem).start()
     pltpu.make_async_copy(wo_hbm, wt.at[rank:2 * rank, feats:], w_sem).start()
-    for group, owners in enumerate(first_group + second_group):
+    starts = [0]
+    for c, owners in enumerate(chunks):
         for k, (xd, zd) in enumerate(owners):
-            s, slot = xd * nz + zd, group * 4 + k
-            pltpu.make_async_copy(x_hbm.at[s], acts.at[slot, :, 0:feats], load_sem.at[group]).start()
-            pltpu.make_async_copy(g_hbm.at[s], acts.at[slot, :, feats:], load_sem.at[group]).start()
+            s, slot = xd * nz + zd, starts[c] + k
+            pltpu.make_async_copy(x_hbm.at[s], acts.at[slot, :, 0:feats], load_sem.at[c]).start()
+            pltpu.make_async_copy(g_hbm.at[s], acts.at[slot, :, feats:], load_sem.at[c]).start()
+        starts.append(starts[c] + len(owners))
     own_q = pltpu.make_async_copy(q_hbm, qall.at[d], own_q_sem)
     own_q.start()
     own_len = pltpu.make_async_copy(len_hbm, len_ref, len_sem)
@@ -83,11 +98,17 @@
     drain(wt.at[0:rank], w_sem)
     w[...] = wt[...].T
 
-    def project(group):
-        block = acts.at[group * 4:group * 4 + 4]
-        drain(block, load_sem.at[group])
-        rows = block[...].reshape(4 * tokens, block.shape[2])
-        return jnp.dot(rows, w[...], preferred_element_type=F32).reshape(4, tokens, 2 * rank)
+    def project(c):
+        count = starts[c + 1] - starts[c]
+        block = acts.at[starts[c]:starts[c + 1]]
+        drain(block, load_sem.at[c])
+        total = jnp.dot(
+            block[:, :, 0:feats].reshape(count * tokens, feats), w[0:feats, :], preferred_element_type=F32
+        )
+        total += jnp.dot(
+            block[:, :, feats:].reshape(count * tokens, block.shape[2] - feats), w[feats:, :], preferred_element_type=F32
+        )
+        return total.reshape(count // 2, 2, tokens, 2 * rank)
 
     def send(src, dst, send_sem, recv_sem, device):
         pltpu.make_async_remote_copy(
@@ -96,59 +117,77 @@
 
     def send_far(i):
         for side, device in enumerate((right, left)):
-            send(sent.at[i, side], chain_in.at[i, side], x_send, chain_recv.at[i, side], device)
+            send(sent.at[0, i, side], chain_in.at[i, side], x_send, chain_recv.at[i, side], device)
 
     def send_raw(i):
-        send(sent.at[i, 2], final_in.at[i, 1, 0], x_send, final_recv.at[i], right)
-        send(sent.at[i, 3], final_in.at[i, 0, 1], x_send, final_recv.at[i], left)
+        send(sent.at[1, i, 0], final_in.at[i, 1, 0], x_send, final_recv.at[i], right)
+        send(sent.at[1, i, 1], final_in.at[i, 0, 1], x_send, final_recv.at[i], left)
 
     def combine(i):
         for side, device in enumerate((right, left)):
             drain(chain_in.at[i, side], chain_recv.at[i, side])
-            sent[i, 4 + side] = encode(keep[i, side] + decode(chain_in[i, side]))
-            send(sent.at[i, 4 + side], final_in.at[i, side, side], x_send, final_recv.at[i], device)
+            sent[2, i, side] = encode(keep[0, i, side] + decode(chain_in[i, side]))
+            send(sent.at[2, i, side], final_in.at[i, side, side], x_send, final_recv.at[i], device)
 
     def reduce_x(i):
         drain(final_in.at[i], final_recv.at[i])
         for parity, k in enumerate(offsets[i]):
-            total = keep[i, 2 + parity] + (decode(final_in[i, parity, 0]) + decode(final_in[i, parity, 1]))
+            total = keep[1, i, parity] + (decode(final_in[i, parity, 0]) + decode(final_in[i, parity, 1]))
             if k == 0:
                 return total
             z_out[k - 1] = encode(total)
-            send(z_out.at[k - 1], z_in.at[k - 1], z_send, z_recv, peer(0, k))
-
-    for i in range(half):
-        sent[i, 0:4] = encode(project(i))
-    pl.semaphore_wait(barrier, len(partners))
-    send_far(0)
-    if half > 1:
-        send_far(1)
+            send(z_out.at[k - 1], z_in.at[k - 1], z_send, z_recv.at[k - 1], peer(0, k))
+
+    def send_queries():
+        for k in range(1, ny):
+            send(q_hbm, qall.at[d], q_send, q_recv, peer_y(k, core))
+
+        @pl.when(core == 1)
+        def _():
+            for k in range(ny):
+                pl.semaphore_signal(in_sem, inc=1, device_id=peer_y(k, 0), device_id_type=MESH)
+                send(q_hbm, qall.at[d], q_send, q_recv, peer_y(k, 0))
+
+    sent[0, 0:early] = encode(project(0))
+    pl.semaphore_wait(barrier, len(partners) + core * ny)
+    for i in range(early):
+        send_far(i)
+    sent[1, 0:early] = encode(project(1))
     send_raw(0)
-    for i in range(2, half):
+    sent[0, early:] = encode(project(2))
+    send_far(early)
+    keep[0] = project(3)
+    combine(0)
+    for i in range(1, early):
+        send_raw(i)
+        combine(i)
+    for i in range(early + 1, half):
         send_far(i)
-        send_raw(i - 1)
-    for i in range(half):
-        keep[i] = project(half + i)
+    sent[1, early:] = encode(project(4))
+    send_raw(early)
+    combine(early)
+    for i in range(early + 1, half):
+        send_raw(i)
+    send_queries()
+    keep[1] = project(5)
+    for i in range(early):
+        reduce_x(i)
+    for i in range(early + 1, half):
         combine(i)
-        if i == 0 and half > 1:
-            send_raw(half - 1)
-        if i == 0:
-            for k in range(1, nd):
-                send(q_hbm, qall.at[d], q_send, q_recv, {"tensor": t, "dp": (d + k) % nd})
-    for i in range(half):
+    for i in range(early, half):
         total = reduce_x(i)
 
-    own_q.wait()
+    @pl.when(core == 0)
+    def _():
+        pl.semaphore_wait(in_sem, ny)
+        for k in range(ny):
+            send(q_hbm, qall.at[d], q_send, q_recv, peer_y(k, 1))
+
+    for k in (k for pair in offsets for k in pair if k > 0):
+        drain(z_in.at[k - 1], z_recv.at[k - 1])
+        total += decode(z_in[k - 1])
+
     own_len.wait()
-    drain(qall.at[0:nd - 1], q_recv)
-    rows = qall.shape[1]
-    for k in range(0, nd, 2):
-        qflat[k * rows:(k + 2) * rows, :] = jnp.concatenate([qall[k], qall[k + 1]], axis=0)
-
-    drain(z_in, z_recv)
-    for k in range(nz - 1):
-        total += decode(z_in[k])
-
     live = (lax.broadcasted_iota(jnp.int32, (tokens, 2 * rank), 0) < len_ref[t]).astype(F32)
     lane = lax.broadcasted_iota(jnp.int32, (tokens, 2 * rank), 1)
     both = jnp.where(lane < rank, pltpu.roll(total, rank, 1), total)
@@ -169,6 +208,13 @@
     for dx, dz in others:
         send(exall.at[t], exall.at[t], ex_send, ex_recv, peer(dx, dz))
     count = exall.shape[0]
+
+    own_q.wait()
+    drain(qall.at[0:nd - 1], q_recv)
+    rows = qall.shape[1]
+    for k in range(0, nd, 2):
+        qflat[k * rows:(k + 2) * rows, :] = jnp.concatenate([qall[k], qall[k + 1]], axis=0)
+
     drain(exall.at[0:count - 1], ex_recv)
 
     exwide[...] = exall[...].reshape(count * pairs, 2 * rank).astype(F32)
@@ -205,8 +251,8 @@
                 pltpu.VMEM((lanes, feats + grads), BF16),
                 pltpu.VMEM((feats + grads, lanes), BF16),
                 pltpu.SMEM(lengths.shape, jnp.int32),
-                pltpu.VMEM((half, 6) + block, BF16),
-                pltpu.VMEM((half, 4) + block, F32),
+                pltpu.VMEM((3, half, 2) + block, BF16),
+                pltpu.VMEM((2, half, 2) + block, F32),
                 pltpu.VMEM((half, 2) + block, BF16),
                 pltpu.VMEM((half, 2, 2) + block, BF16),
                 pltpu.VMEM((nz - 1,) + block, BF16),
@@ -216,8 +262,8 @@
                 pltpu.VMEM((seqs, rank // 2, lanes), BF16),
                 pltpu.VMEM((seqs * rank // 2, lanes), F32),
                 pltpu.VMEM((rank, lanes), F32),
-                dma((nz,)),
-            ] + [dma] * 7 + [dma((half, 2)), dma((half,))] + [dma] * 3,
+                dma((6,)),
+            ] + [dma] * 3 + [pltpu.SemaphoreType.REGULAR] + [dma] * 4 + [dma((half, 2)), dma((half,)), dma((nz - 1,))] + [dma] * 2,
             compiler_params=pltpu.CompilerParams(
                 collective_id=0, has_side_effects=True, vmem_limit_bytes=60 * 1024 * 1024
             ),

time: 37.4 us -> 36.3 us (0.971)
  Pallas kernels: 35.9 us -> 34.8 us
    pallas_call x1, Pallas kernels: 35.9 us -> 34.8 us  [body(): pl.pallas_call(functools.partial(kernel, nz, nd), out_shape=jax.ShapeDtyp...]
where the time goes in v3:
time: 36.3 us; the launch traced here: 36.1 us
  Pallas kernels  34.8 us (96%)
  local copies, waits for them, and re-layouts  1.32 us (4%)
    pallas_call x1, Pallas kernels, body(): pl.pallas_call(functools.partial(kernel, nz, nd), out_shape=jax.ShapeDtyp...  34.8 us
    unnamed x1, local copies, waits for them, and re-layouts  1.32 us

profile of v3, /device:TPU:8, one launch (start us, length us, event | category | flops | bytes accessed | tf_op | source)
XLA Modules:
  0.0 36.1 jit_solution(6978270185741736513)
XLA Ops:
  0.0 34.8 %shard_map.64 = f32[32,64]{1,0:T(8,128)} custom-call(bf16[32,128,896]{2,1,0:T(8,128)(2,1)} %x_hbm.1, bf16[32,128,256]{2,1,0:T(8,128)(2,1)} %g_hbm.1, bf16[64,896]{1,0:T(8,128)(2,1)} %bitcast.2, bf16[64,256]{1,0:T(8,128)(2,1)} %bitcast.3, s32[32]{0:T(128)} %len_hbm.1, bf16[8,4096]{1,0:T(8,128)(2,1)} %q_hbm.1), custom_call_target="tpu_custom_call" | custom-call | tf_op jit(solution)/shard_map/pallas_call | solution.py:244
  34.8 1.3 %copy.8 = f32[32,64]{1,0:T(8,128)} copy(f32[32,64]{1,0:T(8,128)} %shard_map.64) | data formatting | bytes 16384

commit v4 on v3

--- a/solution.py
+++ b/solution.py
@@ -36,7 +36,7 @@
     nz, nd,
     x_hbm, g_hbm, wi_hbm, wo_hbm, len_hbm, q_hbm, out_ref,
     acts, wt, w, len_ref, sent, keep, chain_in, final_in, z_out, z_in, qall, qflat, exall, exwide, small,
-    load_sem, w_sem, len_sem, own_q_sem, in_sem, x_send, z_send, q_send, ex_send, chain_recv, final_recv, z_recv, q_recv, ex_recv,
+    load_sem, w_sem, len_sem, own_q_sem, in_core, in_z, x_send, z_send, q_send, ex_send, chain_recv, final_recv, z_recv, q_recv, ex_recv,
 ):
     half = nz // 2
     tokens, rank = x_hbm.shape[1], wi_hbm.shape[0]
@@ -57,7 +57,6 @@
 
     barrier = pltpu.get_barrier_semaphore()
     partners = [right, left]
-    partners += [peer(0, k) for k in range(1, nz)]
     partners += [peer_y(k, core) for k in range(1, ny)]
     for partner in partners:
         pl.semaphore_signal(barrier, inc=1, device_id=partner, device_id_type=MESH)
@@ -66,14 +65,19 @@
     def _():
         for k in range(ny):
             pl.semaphore_signal(barrier, inc=1, device_id=peer_y(k, 1), device_id_type=MESH)
+
+    for k in range(1, nz):
+        @pl.when(z + k < nz)
+        def _(k=k):
+            pl.semaphore_signal(barrier, inc=1, device_id=peer(0, k), device_id_type=MESH)
 
     offsets = [(half + i, half - 1 - i) for i in range(half)]
     chunks = [[], [], [], [], [], []]
     early = (half + 1) // 2
     for i, (even, odd) in enumerate(offsets):
         ze, zo = (z + even) % nz, (z + odd) % nz
-        chunks[0 if i < early else 2] += [(x_far, ze), (x_far, zo)]
-        chunks[1 if i < early else 4] += [(x_right, zo), (x_left, ze)]
+        chunks[0 if i < early else 1] += [(x_far, ze), (x_far, zo)]
+        chunks[2 if i < early else 4] += [(x_right, zo), (x_left, ze)]
         chunks[3] += [(x_right, ze), (x_left, zo)]
         chunks[5] += [(x, ze), (x, zo)]
 
@@ -145,41 +149,45 @@
         @pl.when(core == 1)
         def _():
             for k in range(ny):
-                pl.semaphore_signal(in_sem, inc=1, device_id=peer_y(k, 0), device_id_type=MESH)
+                pl.semaphore_signal(in_core, inc=1, device_id=peer_y(k, 0), device_id_type=MESH)
                 send(q_hbm, qall.at[d], q_send, q_recv, peer_y(k, 0))
 
     sent[0, 0:early] = encode(project(0))
-    pl.semaphore_wait(barrier, len(partners) + core * ny)
+    pl.semaphore_wait(barrier, len(partners) + core * ny + z)
     for i in range(early):
         send_far(i)
-    sent[1, 0:early] = encode(project(1))
+    for k in range(1, nz):
+        @pl.when(z - k >= 0)
+        def _(k=k):
+            pl.semaphore_signal(in_z, inc=1, device_id=peer(0, nz - k), device_id_type=MESH)
+
+    sent[0, early:] = encode(project(1))
+    for i in range(early, half):
+        send_far(i)
+    sent[1, 0:early] = encode(project(2))
     send_raw(0)
-    sent[0, early:] = encode(project(2))
-    send_far(early)
     keep[0] = project(3)
     combine(0)
     for i in range(1, early):
         send_raw(i)
         combine(i)
-    for i in range(early + 1, half):
-        send_far(i)
     sent[1, early:] = encode(project(4))
-    send_raw(early)
-    combine(early)
-    for i in range(early + 1, half):
+    for i in range(early, half):
         send_raw(i)
+        combine(i)
     send_queries()
     keep[1] = project(5)
-    for i in range(early):
-        reduce_x(i)
-    for i in range(early + 1, half):
-        combine(i)
-    for i in range(early, half):
+
+    @pl.when(z + 1 < nz)
+    def _():
+        pl.semaphore_wait(in_z, nz - 1 - z)
+
+    for i in range(half):
         total = reduce_x(i)
 
     @pl.when(core == 0)
     def _():
-        pl.semaphore_wait(in_sem, ny)
+        pl.semaphore_wait(in_core, ny)
         for k in range(ny):
             send(q_hbm, qall.at[d], q_send, q_recv, peer_y(k, 1))
 
@@ -263,7 +271,7 @@
                 pltpu.VMEM((seqs * rank // 2, lanes), F32),
                 pltpu.VMEM((rank, lanes), F32),
                 dma((6,)),
-            ] + [dma] * 3 + [pltpu.SemaphoreType.REGULAR] + [dma] * 4 + [dma((half, 2)), dma((half,)), dma((nz - 1,))] + [dma] * 2,
+            ] + [dma] * 3 + [pltpu.SemaphoreType.REGULAR] * 2 + [dma] * 4 + [dma((half, 2)), dma((half,)), dma((nz - 1,))] + [dma] * 2,
             compiler_params=pltpu.CompilerParams(
                 collective_id=0, has_side_effects=True, vmem_limit_bytes=60 * 1024 * 1024
             ),

time: 36.3 us -> 34.9 us (0.961)
  Pallas kernels: 34.8 us -> 33.4 us
    pallas_call x1, Pallas kernels: 34.8 us -> 33.4 us  [body(): pl.pallas_call(functools.partial(kernel, nz, nd), out_shape=jax.ShapeDtyp...]
where the time goes in v4:
time: 34.9 us; the launch traced here: 34.8 us
  Pallas kernels  33.4 us (96%)
  local copies, waits for them, and re-layouts  1.32 us (4%)
    pallas_call x1, Pallas kernels, body(): pl.pallas_call(functools.partial(kernel, nz, nd), out_shape=jax.ShapeDtyp...  33.4 us
    unnamed x1, local copies, waits for them, and re-layouts  1.32 us

profile of v4, /device:TPU:8, one launch (start us, length us, event | category | flops | bytes accessed | tf_op | source)
XLA Modules:
  0.0 34.8 jit_solution(6922132253646066230)
XLA Ops:
  0.0 33.4 %shard_map.64 = f32[32,64]{1,0:T(8,128)} custom-call(bf16[32,128,896]{2,1,0:T(8,128)(2,1)} %x_hbm.1, bf16[32,128,256]{2,1,0:T(8,128)(2,1)} %g_hbm.1, bf16[64,896]{1,0:T(8,128)(2,1)} %bitcast.2, bf16[64,256]{1,0:T(8,128)(2,1)} %bitcast.3, s32[32]{0:T(128)} %len_hbm.1, bf16[8,4096]{1,0:T(8,128)(2,1)} %q_hbm.1), custom_call_target="tpu_custom_call" | custom-call | tf_op jit(solution)/shard_map/pallas_call | solution.py:252
  33.4 1.3 %copy.8 = f32[32,64]{1,0:T(8,128)} copy(f32[32,64]{1,0:T(8,128)} %shard_map.64) | data formatting | bytes 16384

commit v5 on v4

--- a/solution.py
+++ b/solution.py
@@ -152,7 +152,22 @@
                 pl.semaphore_signal(in_core, inc=1, device_id=peer_y(k, 0), device_id_type=MESH)
                 send(q_hbm, qall.at[d], q_send, q_recv, peer_y(k, 0))
 
-    sent[0, 0:early] = encode(project(0))
+    def place(c):
+        if c == 0:
+            sent[0, 0:early] = encode(project(c))
+        elif c == 1:
+            sent[0, early:] = encode(project(c))
+        elif c == 2:
+            sent[1, 0:early] = encode(project(c))
+        elif c == 4:
+            sent[1, early:] = encode(project(c))
+        else:
+            keep[(c - 3) // 2] = project(c)
+
+    def block(c):
+        pl.when(core >= 0)(lambda: place(c))
+
+    block(0)
     pl.semaphore_wait(barrier, len(partners) + core * ny + z)
     for i in range(early):
         send_far(i)
@@ -161,22 +176,22 @@
         def _(k=k):
             pl.semaphore_signal(in_z, inc=1, device_id=peer(0, nz - k), device_id_type=MESH)
 
-    sent[0, early:] = encode(project(1))
+    block(1)
     for i in range(early, half):
         send_far(i)
-    sent[1, 0:early] = encode(project(2))
+    block(2)
     send_raw(0)
-    keep[0] = project(3)
+    block(3)
     combine(0)
     for i in range(1, early):
         send_raw(i)
         combine(i)
-    sent[1, early:] = encode(project(4))
+    block(4)
     for i in range(early, half):
         send_raw(i)
         combine(i)
     send_queries()
-    keep[1] = project(5)
+    block(5)
 
     @pl.when(z + 1 < nz)
     def _():
@@ -251,7 +266,7 @@
         dma = pltpu.SemaphoreType.DMA
         return pl.pallas_call(
             functools.partial(kernel, nz, nd),
-            out_shape=jax.ShapeDtypeStruct((seqs, nd * queries.shape[0]), F32),
+            out_shape=pltpu.VMEM((seqs, nd * queries.shape[0]), F32),
             in_specs=[pl.BlockSpec(memory_space=pltpu.HBM)] * 6,
             out_specs=pl.BlockSpec(memory_space=pltpu.VMEM),
             scratch_shapes=[
@@ -275,7 +290,10 @@
             compiler_params=pltpu.CompilerParams(
                 collective_id=0, has_side_effects=True, vmem_limit_bytes=60 * 1024 * 1024
             ),
-        )(inputs, out_grads, proj_in.T, proj_out.T, lengths, queries)
+        )(*(
+            pltpu.with_memory_space_constraint(operand, pltpu.HBM)
+            for operand in (inputs, out_grads, proj_in.T, proj_out.T, lengths, queries)
+        ))
 
     return jax.shard_map(
         body,

time: 34.9 us -> 33.3 us (0.954)
  Pallas kernels: 33.4 us -> 32.6 us
  local copies, waits for them, and re-layouts: 1.32 us -> 0.61 us
    pallas_call x1, Pallas kernels: 33.4 us -> 32.6 us  [body(): pl.pallas_call(functools.partial(kernel, nz, nd), out_shape=pltpu.VMEM((s...]
    unnamed x1, local copies, waits for them, and re-layouts: 1.32 us -> 0.61 us
where the time goes in v5:
time: 33.3 us; the launch traced here: 33.2 us
  Pallas kernels  32.6 us (98%)
  local copies, waits for them, and re-layouts  0.61 us (2%)
    pallas_call x1, Pallas kernels, body(): pl.pallas_call(functools.partial(kernel, nz, nd), out_shape=pltpu.VMEM((s...  32.6 us

profile of v5, /device:TPU:8, one launch (start us, length us, event | category | flops | bytes accessed | tf_op | source)
XLA Modules:
  0.0 33.2 jit_solution(10413453584673778981)
XLA Ops:
  0.0 32.6 %shard_map.64 = f32[32,64]{1,0:T(8,128)S(1)} custom-call(bf16[32,128,896]{2,1,0:T(8,128)(2,1)} %x_hbm.1, bf16[32,128,256]{2,1,0:T(8,128)(2,1)} %g_hbm.1, bf16[64,896]{1,0:T(8,128)(2,1)} %bitcast.2, bf16[64,256]{1,0:T(8,128)(2,1)} %bitcast.3, s32[32]{0:T(128)} %len_hbm.1, bf16[8,4096]{1,0:T(8,128)(2,1)} %q_hbm.1), custom_call_target="tpu_custom_call" | custom-call | tf_op jit(solution)/shard_map/pallas_call | solution.py:267
  32.6 0.6 %copy.8 = f32[32,64]{1,0:T(8,128)} copy(f32[32,64]{1,0:T(8,128)S(1)} %shard_map.64) | data formatting | bytes 16384

commit v6 on v5

--- a/solution.py
+++ b/solution.py
@@ -36,7 +36,7 @@
     nz, nd,
     x_hbm, g_hbm, wi_hbm, wo_hbm, len_hbm, q_hbm, out_ref,
     acts, wt, w, len_ref, sent, keep, chain_in, final_in, z_out, z_in, qall, qflat, exall, exwide, small,
-    load_sem, w_sem, len_sem, own_q_sem, in_core, in_z, x_send, z_send, q_send, ex_send, chain_recv, final_recv, z_recv, q_recv, ex_recv,
+    load_sem, w_sem, len_sem, own_q_sem, in_z, x_send, z_send, q_send, ex_send, chain_recv, final_recv, z_recv, ex_recv, q_recv,
 ):
     half = nz // 2
     tokens, rank = x_hbm.shape[1], wi_hbm.shape[0]
@@ -55,16 +55,17 @@
     def peer_y(dy, side):
         return {"tensor": t, "dp": ((y + dy) % ny) * 2 + side}
 
+    near_y = sorted({1, ny - 1} - {0}) if ny > 1 else []
+    far_y = [k for k in range(1, ny) if k not in near_y]
     barrier = pltpu.get_barrier_semaphore()
     partners = [right, left]
-    partners += [peer_y(k, core) for k in range(1, ny)]
+    partners += [peer_y(k, core) for k in near_y]
     for partner in partners:
         pl.semaphore_signal(barrier, inc=1, device_id=partner, device_id_type=MESH)
 
     @pl.when(core == 0)
     def _():
-        for k in range(ny):
-            pl.semaphore_signal(barrier, inc=1, device_id=peer_y(k, 1), device_id_type=MESH)
+        pl.semaphore_signal(barrier, inc=1, device_id=peer_y(0, 1), device_id_type=MESH)
 
     for k in range(1, nz):
         @pl.when(z + k < nz)
@@ -74,9 +75,10 @@
     offsets = [(half + i, half - 1 - i) for i in range(half)]
     chunks = [[], [], [], [], [], []]
     early = (half + 1) // 2
+    first = max(half // 4, 1)
     for i, (even, odd) in enumerate(offsets):
         ze, zo = (z + even) % nz, (z + odd) % nz
-        chunks[0 if i < early else 1] += [(x_far, ze), (x_far, zo)]
+        chunks[0 if i < first else 1] += [(x_far, ze), (x_far, zo)]
         chunks[2 if i < early else 4] += [(x_right, zo), (x_left, ze)]
         chunks[3] += [(x_right, ze), (x_left, zo)]
         chunks[5] += [(x, ze), (x, zo)]
@@ -142,21 +144,63 @@
             z_out[k - 1] = encode(total)
             send(z_out.at[k - 1], z_in.at[k - 1], z_send, z_recv.at[k - 1], peer(0, k))
 
-    def send_queries():
-        for k in range(1, ny):
-            send(q_hbm, qall.at[d], q_send, q_recv, peer_y(k, core))
-
-        @pl.when(core == 1)
-        def _():
-            for k in range(ny):
-                pl.semaphore_signal(in_core, inc=1, device_id=peer_y(k, 0), device_id_type=MESH)
-                send(q_hbm, qall.at[d], q_send, q_recv, peer_y(k, 0))
+    def send_query(k, side):
+        send(q_hbm, qall.at[d], q_send, q_recv.at[(core + side) % 2, k], peer_y(k, side))
+
+    def take_query(k, side):
+        drain(qall.at[0], q_recv.at[(core + side) % 2, k])
+
+    def on(side):
+        return pl.when(core == side)
+
+    def first_queries():
+        for k in near_y:
+            send_query(k, core)
+        on(1)(lambda: send_query(0, 0))
+
+    def second_queries():
+        for k in near_y:
+            take_query(k, core)
+        for k in far_y:
+            send_query(k, core)
+
+        @on(1)
+        def _():
+            for k in near_y:
+                send_query(k, 0)
+
+    def third_queries():
+        for k in far_y:
+            take_query(k, core)
+
+        @on(1)
+        def _():
+            for k in far_y:
+                send_query(k, 0)
+
+        @on(0)
+        def _():
+            for k in [0] + near_y:
+                take_query(k, 1)
+                send_query((ny - k) % ny, 1)
+
+    def last_queries():
+        @on(0)
+        def _():
+            for k in far_y:
+                take_query(k, 1)
+                send_query((ny - k) % ny, 1)
+
+        @on(1)
+        def _():
+            for k in [0] + near_y + far_y:
+                take_query(k, 0)
 
     def place(c):
         if c == 0:
-            sent[0, 0:early] = encode(project(c))
+            sent[0, 0:first] = encode(project(c))
         elif c == 1:
-            sent[0, early:] = encode(project(c))
+            sent[0, first:] = encode(project(c))
         elif c == 2:
             sent[1, 0:early] = encode(project(c))
         elif c == 4:
@@ -168,8 +212,8 @@
         pl.when(core >= 0)(lambda: place(c))
 
     block(0)
-    pl.semaphore_wait(barrier, len(partners) + core * ny + z)
-    for i in range(early):
+    pl.semaphore_wait(barrier, len(partners) + core + z)
+    for i in range(first):
         send_far(i)
     for k in range(1, nz):
         @pl.when(z - k >= 0)
@@ -177,10 +221,11 @@
             pl.semaphore_signal(in_z, inc=1, device_id=peer(0, nz - k), device_id_type=MESH)
 
     block(1)
-    for i in range(early, half):
+    for i in range(first, half):
         send_far(i)
     block(2)
     send_raw(0)
+    first_queries()
     block(3)
     combine(0)
     for i in range(1, early):
@@ -190,7 +235,7 @@
     for i in range(early, half):
         send_raw(i)
         combine(i)
-    send_queries()
+    second_queries()
     block(5)
 
     @pl.when(z + 1 < nz)
@@ -200,12 +245,7 @@
     for i in range(half):
         total = reduce_x(i)
 
-    @pl.when(core == 0)
-    def _():
-        pl.semaphore_wait(in_core, ny)
-        for k in range(ny):
-            send(q_hbm, qall.at[d], q_send, q_recv, peer_y(k, 1))
-
+    third_queries()
     for k in (k for pair in offsets for k in pair if k > 0):
         drain(z_in.at[k - 1], z_recv.at[k - 1])
         total += decode(z_in[k - 1])
@@ -233,7 +273,7 @@
     count = exall.shape[0]
 
     own_q.wait()
-    drain(qall.at[0:nd - 1], q_recv)
+    last_queries()
     rows = qall.shape[1]
     for k in range(0, nd, 2):
         qflat[k * rows:(k + 2) * rows, :] = jnp.concatenate([qall[k], qall[k + 1]], axis=0)
@@ -286,7 +326,7 @@
                 pltpu.VMEM((seqs * rank // 2, lanes), F32),
                 pltpu.VMEM((rank, lanes), F32),
                 dma((6,)),
-            ] + [dma] * 3 + [pltpu.SemaphoreType.REGULAR] * 2 + [dma] * 4 + [dma((half, 2)), dma((half,)), dma((nz - 1,))] + [dma] * 2,
+            ] + [dma] * 3 + [pltpu.SemaphoreType.REGULAR] + [dma] * 4 + [dma((half, 2)), dma((half,)), dma((nz - 1,))] + [dma, dma((2, nd // 2))],
             compiler_params=pltpu.CompilerParams(
                 collective_id=0, has_side_effects=True, vmem_limit_bytes=60 * 1024 * 1024
             ),

time: 33.3 us -> 33.5 us (level)
  no operation moved by 1% of the time
where the time goes in v6:
time: 33.5 us; the launch traced here: 33.2 us
  Pallas kernels  32.6 us (97%)
  local copies, waits for them, and re-layouts  0.61 us (2%)
    pallas_call x1, Pallas kernels, body(): pl.pallas_call(functools.partial(kernel, nz, nd), out_shape=pltpu.VMEM((s...  32.6 us

profile of v6, /device:TPU:8, one launch (start us, length us, event | category | flops | bytes accessed | tf_op | source)
XLA Modules:
  0.0 33.2 jit_solution(1931961548760481066)
XLA Ops:
  0.0 32.6 %shard_map.64 = f32[32,64]{1,0:T(8,128)S(1)} custom-call(bf16[32,128,896]{2,1,0:T(8,128)(2,1)} %x_hbm.1, bf16[32,128,256]{2,1,0:T(8,128)(2,1)} %g_hbm.1, bf16[64,896]{1,0:T(8,128)(2,1)} %bitcast.2, bf16[64,256]{1,0:T(8,128)(2,1)} %bitcast.3, s32[32]{0:T(128)} %len_hbm.1, bf16[8,4096]{1,0:T(8,128)(2,1)} %q_hbm.1), custom_call_target="tpu_custom_call" | custom-call | tf_op jit(solution)/shard_map/pallas_call | solution.py:307
  32.6 0.6 %copy.8 = f32[32,64]{1,0:T(8,128)} copy(f32[32,64]{1,0:T(8,128)S(1)} %shard_map.64) | data formatting | bytes 16384

commit v7 on v6

--- a/solution.py
+++ b/solution.py
@@ -83,25 +83,31 @@
         chunks[3] += [(x_right, ze), (x_left, zo)]
         chunks[5] += [(x, ze), (x, zo)]
 
+    starts = [0]
+    for owners in chunks:
+        starts.append(starts[-1] + len(owners))
+
+    def load(c):
+        for k, (xd, zd) in enumerate(chunks[c]):
+            s, slot = xd * nz + zd, starts[c] + k
+            pltpu.make_async_copy(x_hbm.at[s], acts.at[slot, :, 0:feats], load_sem.at[c]).start()
+            pltpu.make_async_copy(g_hbm.at[s], acts.at[slot, :, feats:], load_sem.at[c]).start()
+
+    own_q = pltpu.make_async_copy(q_hbm, qall.at[d], own_q_sem)
+    own_len = pltpu.make_async_copy(len_hbm, len_ref, len_sem)
     wt[...] = jnp.zeros_like(wt)
     pltpu.make_async_copy(wi_hbm, wt.at[0:rank, 0:feats], w_sem).start()
     pltpu.make_async_copy(wo_hbm, wt.at[rank:2 * rank, feats:], w_sem).start()
-    starts = [0]
-    for c, owners in enumerate(chunks):
-        for k, (xd, zd) in enumerate(owners):
-            s, slot = xd * nz + zd, starts[c] + k
-            pltpu.make_async_copy(x_hbm.at[s], acts.at[slot, :, 0:feats], load_sem.at[c]).start()
-            pltpu.make_async_copy(g_hbm.at[s], acts.at[slot, :, feats:], load_sem.at[c]).start()
-        starts.append(starts[c] + len(owners))
-    own_q = pltpu.make_async_copy(q_hbm, qall.at[d], own_q_sem)
-    own_q.start()
-    own_len = pltpu.make_async_copy(len_hbm, len_ref, len_sem)
-    own_len.start()
+    load(0)
 
     def drain(ref, sem):
         pltpu.make_async_copy(ref, ref, sem).wait()
 
     drain(wt.at[0:rank], w_sem)
+    for c in range(1, len(chunks)):
+        load(c)
+    own_q.start()
+    own_len.start()
     w[...] = wt[...].T
 
     def project(c):

time: 33.5 us -> 31.7 us (0.946)
  the two profiles are of different devices: /device:TPU:8 before, /device:TPU:32 now
where the time goes in v7:
time: 31.7 us; the launch traced here: 31.6 us
  Pallas kernels  31 us (98%)
  local copies, waits for them, and re-layouts  0.61 us (2%)
    pallas_call x1, Pallas kernels, body(): pl.pallas_call(functools.partial(kernel, nz, nd), out_shape=pltpu.VMEM((s...  31 us

profile of v7, /device:TPU:32, one launch (start us, length us, event | category | flops | bytes accessed | tf_op | source)
XLA Modules:
  0.0 31.6 jit_solution(7944165259941675921)
XLA Ops:
  0.0 31.0 %shard_map.64 = f32[32,64]{1,0:T(8,128)S(1)} custom-call(bf16[32,128,896]{2,1,0:T(8,128)(2,1)} %x_hbm.1, bf16[32,128,256]{2,1,0:T(8,128)(2,1)} %g_hbm.1, bf16[64,896]{1,0:T(8,128)(2,1)} %bitcast.2, bf16[64,256]{1,0:T(8,128)(2,1)} %bitcast.3, s32[32]{0:T(128)} %len_hbm.1, bf16[8,4096]{1,0:T(8,128)(2,1)} %q_hbm.1), custom_call_target="tpu_custom_call" | custom-call | tf_op jit(solution)/shard_map/pallas_call | solution.py:313
  31.0 0.6 %copy.8 = f32[32,64]{1,0:T(8,128)} copy(f32[32,64]{1,0:T(8,128)S(1)} %shard_map.64) | data formatting | bytes 16384

commit v8 on v7

--- a/solution.py
+++ b/solution.py
@@ -13,13 +13,17 @@
 NX = 4
 
 
+SCALE = 2.0**50
+
+
 def encode(value):
-    return (value * jnp.abs(value)).astype(BF16)
+    scaled = value * SCALE
+    return (scaled * jnp.abs(scaled)).astype(BF16)
 
 
 def decode(code):
     wide = code.astype(F32)
-    root = jnp.sqrt(jnp.abs(wide))
+    root = jnp.sqrt(jnp.abs(wide)) * (1.0 / SCALE)
     return jnp.where(wide < 0, -root, root)
 
 

time: 31.7 us -> 31.7 us (level)
  no operation moved by 1% of the time
where the time goes in v8:
time: 31.7 us; the launch traced here: 31.6 us
  Pallas kernels  31 us (98%)
  local copies, waits for them, and re-layouts  0.61 us (2%)
    pallas_call x1, Pallas kernels, body(): pl.pallas_call(functools.partial(kernel, nz, nd), out_shape=pltpu.VMEM((s...  31 us

profile of v8, /device:TPU:32, one launch (start us, length us, event | category | flops | bytes accessed | tf_op | source)
XLA Modules:
  0.0 31.6 jit_solution(407803437700480368)
XLA Ops:
  0.0 31.0 %shard_map.64 = f32[32,64]{1,0:T(8,128)S(1)} custom-call(bf16[32,128,896]{2,1,0:T(8,128)(2,1)} %x_hbm.1, bf16[32,128,256]{2,1,0:T(8,128)(2,1)} %g_hbm.1, bf16[64,896]{1,0:T(8,128)(2,1)} %bitcast.2, bf16[64,256]{1,0:T(8,128)(2,1)} %bitcast.3, s32[32]{0:T(128)} %len_hbm.1, bf16[8,4096]{1,0:T(8,128)(2,1)} %q_hbm.1), custom_call_target="tpu_custom_call" | custom-call | tf_op jit(solution)/shard_map/pallas_call | solution.py:317
  31.0 0.6 %copy.8 = f32[32,64]{1,0:T(8,128)} copy(f32[32,64]{1,0:T(8,128)S(1)} %shard_map.64) | data formatting | bytes 16384

commit v9 on v8

--- a/solution.py
+++ b/solution.py
@@ -267,10 +267,12 @@
     a_high, a_low = split(total * live)
     b_high, b_low = split(both)
 
-    def outer(left_side, right_side):
-        return lax.dot_general(left_side, right_side, (((0,), (0,)), ((), ())), preferred_element_type=F32)
-
-    small[...] = (outer(a_high, b_high) + (outer(a_high, b_low) + outer(a_low, b_high)))[0:rank]
+    small[...] = lax.dot_general(
+        jnp.concatenate([a_high, a_high, a_low], axis=0),
+        jnp.concatenate([b_high, b_low, b_high], axis=0),
+        (((0,), (0,)), ((), ())),
+        preferred_element_type=F32,
+    )[0:rank]
     pairs = rank // 2
     lane_half = lax.broadcasted_iota(jnp.int32, (pairs, 2 * rank), 1)
     example = jnp.where(lane_half < rank, small[pl.ds(0, pairs, stride=2), :], small[pl.ds(1, pairs, stride=2), :])
@@ -279,7 +281,7 @@
     others = [(dx, dz) for dx in range(NX) for dz in range(nz) if (dx, dz) != (0, 0)]
     others.sort(key=lambda step: -(hops(step[0], NX) + hops(step[1], nz)))
     for dx, dz in others:
-        send(exall.at[t], exall.at[t], ex_send, ex_recv, peer(dx, dz))
+        send(exall.at[t], exall.at[t], ex_send, ex_recv, peer(dx, dz * (1 - core) + (nz - dz) * core))
     count = exall.shape[0]
 
     own_q.wait()

time: 31.7 us -> 31.7 us (level)
  no operation moved by 1% of the time
where the time goes in v9:
time: 31.7 us; the launch traced here: 31.6 us
  Pallas kernels  31 us (98%)
  local copies, waits for them, and re-layouts  0.61 us (2%)
    pallas_call x1, Pallas kernels, body(): pl.pallas_call(functools.partial(kernel, nz, nd), out_shape=pltpu.VMEM((s...  31 us

profile of v9, /device:TPU:32, one launch (start us, length us, event | category | flops | bytes accessed | tf_op | source)
XLA Modules:
  0.0 31.6 jit_solution(3465494447366395866)
XLA Ops:
  0.0 31.0 %shard_map.64 = f32[32,64]{1,0:T(8,128)S(1)} custom-call(bf16[32,128,896]{2,1,0:T(8,128)(2,1)} %x_hbm.1, bf16[32,128,256]{2,1,0:T(8,128)(2,1)} %g_hbm.1, bf16[64,896]{1,0:T(8,128)(2,1)} %bitcast.2, bf16[64,256]{1,0:T(8,128)(2,1)} %bitcast.3, s32[32]{0:T(128)} %len_hbm.1, bf16[8,4096]{1,0:T(8,128)(2,1)} %q_hbm.1), custom_call_target="tpu_custom_call" | custom-call | tf_op jit(solution)/shard_map/pallas_call | solution.py:319
  31.0 0.6 %copy.8 = f32[32,64]{1,0:T(8,128)} copy(f32[32,64]{1,0:T(8,128)S(1)} %shard_map.64) | data formatting | bytes 16384
